TPU v7x, 32 devices: a whole 2x2x4 slice. The times are simulated.
32 devices in a mesh: row: 16 (over z, x, core), col: 2 (over y).
Axes of the slice: x: 2, y: 2, z: 4, core: 2. Of those that a mesh axis runs over, the one named last changes fastest.
Arguments:
- density: bfloat16 [6144, 6144], P('col', 'row'), may hold values from -1.5 to 1.5
- block_mask: int32 [48, 48], replicated, may hold values from 0 to 1, as said below
- owner: int32 [4, 2], replicated, may hold values from 0 to 15, as said below
Outputs:
- square_part: float32 [6144, 6144], P('col', 'row')
Inputs may be any that keep to these rules, and one draw needn't show every extreme that they name: owner[t, g] // 8 equals (g + t) mod 2. `block_mask`: each tile of 24 x 3 blocks (block rows g * 24 onward, block columns j * 3 onward) has at most 43 entries equal to 1, and in every draw some tile has exactly 43.
All inputs are finite; a program needn't handle non-finite values.
Results may differ from a plain program's by a relative error of at most 0.0003.
Values may be sent and summed in bfloat16 or wider, within the bound.
No kernel may reach another device: no remote copies, remote signals or barrier semaphores. Data moves between devices by JAX's collectives and lax.ppermute only.
A program may use at most 64 MiB of HBM per device.

v0:
```python
import jax
import jax.numpy as jnp
from jax import lax
from jax.sharding import PartitionSpec as P

BLOCK = 128
STEPS = 4


def shifted(x, axis, by):
    devices = lax.axis_size(axis)
    return lax.ppermute(x, axis, [(i, (i + by) % devices) for i in range(devices)])


def from_root(block, axis, source):
    block = jnp.where(lax.axis_index(axis) == source, block, jnp.zeros_like(block))
    return lax.psum(block, axis)


def shards(density, block_mask, owner):
    row_count = lax.axis_size("row")
    col_count = lax.axis_size("col")
    grid_row = lax.axis_index("col")
    grid_col = lax.axis_index("row")
    tile_rows, tile_width = density.shape
    row_blocks = tile_rows // BLOCK
    col_blocks = tile_width // BLOCK
    sub_count = row_count // col_count
    own_mask = lax.dynamic_slice(
        block_mask, (grid_row * row_blocks, grid_col * col_blocks), (row_blocks, col_blocks)
    )
    shaped = density.reshape(row_blocks, BLOCK, col_blocks, BLOCK)
    kept = jnp.where(own_mask[:, None, :, None] == 1, shaped, jnp.zeros((), jnp.bfloat16))
    masked = kept.reshape(tile_rows, tile_width)
    accumulated = jnp.zeros((tile_rows, tile_width), jnp.float32)
    held_tile = masked
    for section_index in range(STEPS):
        root_index = owner[section_index, grid_row]
        slab_index = root_index % sub_count
        if section_index > 0:
            held_tile = shifted(held_tile, "col", -1)
        right_slab = lax.dynamic_slice_in_dim(held_tile, slab_index * tile_width, tile_width, 0)
        left_tile = from_root(masked, "row", root_index)
        accumulated = accumulated + jnp.dot(
            left_tile, right_slab, preferred_element_type=jnp.float32
        )
    return accumulated


def solution(mesh):
    placed = (P("col", "row"), P(), P())
    return jax.shard_map(
        shards, mesh=mesh, in_specs=placed, out_specs=P("col", "row"), check_vma=False
    )
```

profile of v0, /device:TPU:13, one launch (start us, length us, event | category | flops | bytes accessed | tf_op | source)
XLA Modules:
  0.0 231.9 jit_solution(14574365599048165120)
XLA Ops:
  6.5 0.0 all-reduce.3.cloned.1.call-start
  6.5 0.8 dynamic_slice.28
  7.3 0.1 copy.8
  7.4 1.5 constant_dynamic-slice_fusion.1
  9.6 4.3 %copy.7 = bf16[3072,384]{0,1:T(8,128)(2,1)} copy(bf16[3072,384]{1,0:T(8,128)(2,1)} %param.3) | data formatting | bytes 4718592 | tf_op args[0]
  13.9 0.4 broadcast_in_dim.15
  14.3 3.8 %broadcast_select_fusion = (bf16[3072,384]{0,1:T(8,128)(2,1)}, bf16[3072,384]{0,1:T(8,128)(2,1)S(1)}) fusion(pred[]{:T(512)S(6)} %eq.29, bf16[3072,384]{0,1:T(8,128)(2,1)} %copy.7, pred[48,8,24,128]{3,2,1,0:T(8,128)(4,1)S(1)} %bitcast.15), kind=kLoop, calls=%fused_computation.2 | loop fusion | flops 2359296 | bytes 8257537 | tf_op jit(solution)/shard_map/jit(_where)/select_n | solution.py:16
  18.0 0.2 collective-permute-start
  20.0 3.0 %broadcast_select_fusion.2 = (bf16[3072,384]{0,1:T(8,128)(2,1)}, bf16[3072,384]{0,1:T(8,128)(2,1)}, bf16[3072,384]{0,1:T(8,128)(2,1)}) fusion(bf16[3072,384]{0,1:T(8,128)(2,1)S(1)} %get-tuple-element.10, pred[]{:T(512)S(6)} %eq.27, pred[]{:T(512)S(6)} %eq.28, pred[]{:T(512)S(6)} %eq.24), kind=kLoop, calls=%fused_computation.4 | loop fusion | flops 3538944 | bytes 9437187 | tf_op jit(solution)/shard_map/jit(_where)/select_n | solution.py:16
  23.1 0.0 all-reduce.3.cloned.1.call-update
  23.1 47.1 %collective-permute-done = bf16[3072,384]{0,1:T(8,128)(2,1)} collective-permute-done((bf16[3072,384]{0,1:T(8,128)(2,1)S(1)}, bf16[3072,384]{0,1:T(8,128)(2,1)}, u32[]{:S(2)}, u32[]{:S(2)}) %collective-permute-start) | collective-permute-done | bytes 2359328 | tf_op jit(solution)/shard_map/ppermute | solution.py:12
  70.2 0.2 collective-permute-start.1
  70.5 51.3 %collective-permute-done.1 = bf16[3072,384]{0,1:T(8,128)(2,1)} collective-permute-done((bf16[3072,384]{0,1:T(8,128)(2,1)}, bf16[3072,384]{0,1:T(8,128)(2,1)}, u32[]{:S(2)}, u32[]{:S(2)}) %collective-permute-start.1) | collective-permute-done | bytes 2359328 | tf_op jit(solution)/shard_map/ppermute | solution.py:12
  121.8 0.2 collective-permute-start.2
  129.5 81.1 %all-reduce.3.cloned.1.call-done = (bf16[3072,384]{0,1:T(8,128)(2,1)}, bf16[3072,384]{0,1:T(8,128)(2,1)}, bf16[3072,384]{0,1:T(8,128)(2,1)}, bf16[3072,384]{0,1:T(8,128)(2,1)}) async-done(((bf16[3072,384]{0,1:T(8,128)(2,1)}, bf16[3072,384]{0,1:T(8,128)(2,1)}, bf16[3072,384]{0,1:T(8,128)(2,1)}, bf16[3072,384]{0,1:T(8,128)(2,1)}), (bf16[3072,384]{0,1:T(8,128)(2,1)}, bf16[3072,384]{0,1:T(8,128)(2,1)}, ...) | async-done | bytes 9437200 | tf_op jit(solution)/shard_map/psum | solution.py:17
  210.6 0.0 copy-start.1
  210.6 3.5 %fusion.5 = f32[3072,384]{1,0:T(8,128)S(1)} fusion(bf16[3072,384]{0,1:T(8,128)(2,1)} %get-tuple-element.6, bf16[3072,384]{0,1:T(8,128)(2,1)S(1)} %get-tuple-element.10, s32[]{:T(128)S(6)} %select_n.81), kind=kOutput, calls=%fused_computation.11 | convolution fusion | flops 905969664 | bytes 7372804 | tf_op jit(solution)/shard_map/dot_general | solution.py:44
  214.0 0.0 copy-done.1
  214.1 0.0 copy-start
  214.1 2.8 %fusion.3 = f32[3072,384]{1,0:T(8,128)S(1)} fusion(bf16[3072,384]{0,1:T(8,128)(2,1)S(1)} %copy-done.1, bf16[3072,384]{0,1:T(8,128)(2,1)} %collective-permute-done, s32[]{:T(128)S(6)} %select_n.85), kind=kOutput, calls=%fused_computation.9 | convolution fusion | flops 905969664 | bytes 7372804 | tf_op jit(solution)/shard_map/dot_general | solution.py:44
  216.9 0.0 copy-done
  216.9 0.0 copy-start.2
  216.9 2.8 %fusion.1 = f32[3072,384]{1,0:T(8,128)S(1)} fusion(bf16[3072,384]{0,1:T(8,128)(2,1)S(1)} %copy-done, bf16[3072,384]{0,1:T(8,128)(2,1)} %collective-permute-done.1, s32[]{:T(128)S(6)} %select_n.89), kind=kOutput, calls=%fused_computation.7 | convolution fusion | flops 905969664 | bytes 7372804 | tf_op jit(solution)/shard_map/dot_general | solution.py:44
  219.7 0.0 collective-permute-done.2
  219.7 0.0 copy-done.2
  219.7 5.3 %add_add_fusion = f32[3072,384]{1,0:T(8,128)} fusion(f32[3072,384]{1,0:T(8,128)S(1)} %fusion.1, f32[3072,384]{1,0:T(8,128)S(1)} %fusion.5, f32[3072,384]{1,0:T(8,128)S(1)} %fusion.3, bf16[3072,384]{0,1:T(8,128)(2,1)S(1)} %copy-done.2, bf16[3072,384]{0,1:T(8,128)(2,1)} %collective-permute-done.2, s32[]{:T(128)S(6)} %select_n.93), kind=kOutput, calls=%fused_computation | convolution fusion | flops 909508608 | bytes 21528580 | tf_op jit(solution)/shard_map/dot_general | solution.py:44
  (1 shorter events, 0.0 us)
Async XLA Ops:
  6.5 204.0 %all-reduce.3.cloned.1.call-start = ((), (), s32[]{:S(2)}) async-start(), calls=%async_computation | async-start | bytes 18874368 | tf_op jit(solution)/shard_map/psum | solution.py:17
  18.0 52.2 %collective-permute-start = (bf16[3072,384]{0,1:T(8,128)(2,1)S(1)}, bf16[3072,384]{0,1:T(8,128)(2,1)}, u32[]{:S(2)}, u32[]{:S(2)}) collective-permute-start(bf16[3072,384]{0,1:T(8,128)(2,1)S(1)} %get-tuple-element.10), channel_id=1, source_target_pairs={{0,1},{1,0},{2,3},{3,2},{4,5},{5,4},{6,7},{7,6},{8,9},{9,8},{10,11... | collective-permute-start | bytes 7077896 | tf_op jit(solution)/shard_map/ppermute | solution.py:12
  70.2 51.5 %collective-permute-start.1 = (bf16[3072,384]{0,1:T(8,128)(2,1)}, bf16[3072,384]{0,1:T(8,128)(2,1)}, u32[]{:S(2)}, u32[]{:S(2)}) collective-permute-start(bf16[3072,384]{0,1:T(8,128)(2,1)} %collective-permute-done), channel_id=1, source_target_pairs={{0,1},{1,0},{2,3},{3,2},{4,5},{5,4},{6,7},{7,6},{8,9},{9,8},{10,11... | collective-permute-start | bytes 7077896 | tf_op jit(solution)/shard_map/ppermute | solution.py:12
  121.8 98.0 %collective-permute-start.2 = (bf16[3072,384]{0,1:T(8,128)(2,1)}, bf16[3072,384]{0,1:T(8,128)(2,1)}, u32[]{:S(2)}, u32[]{:S(2)}) collective-permute-start(bf16[3072,384]{0,1:T(8,128)(2,1)} %collective-permute-done.1), channel_id=1, source_target_pairs={{0,1},{1,0},{2,3},{3,2},{4,5},{5,4},{6,7},{7,6},{8,9},{9,8},{10,11... | collective-permute-start | bytes 7077896 | tf_op jit(solution)/shard_map/ppermute | solution.py:12
  210.6 3.5 %copy-start.1 = (bf16[3072,384]{0,1:T(8,128)(2,1)S(1)}, bf16[3072,384]{0,1:T(8,128)(2,1)}, u32[]{:S(2)}) copy-start(bf16[3072,384]{0,1:T(8,128)(2,1)} %get-tuple-element.7) | copy-start | bytes 7077892
  214.1 2.8 %copy-start = (bf16[3072,384]{0,1:T(8,128)(2,1)S(1)}, bf16[3072,384]{0,1:T(8,128)(2,1)}, u32[]{:S(2)}) copy-start(bf16[3072,384]{0,1:T(8,128)(2,1)} %get-tuple-element.5) | copy-start | bytes 7077892
  216.9 2.8 %copy-start.2 = (bf16[3072,384]{0,1:T(8,128)(2,1)S(1)}, bf16[3072,384]{0,1:T(8,128)(2,1)}, u32[]{:S(2)}) copy-start(bf16[3072,384]{0,1:T(8,128)(2,1)} %get-tuple-element.8) | copy-start | bytes 7077892
Sparse Core Ops, SparseCore 0:
  23.2 187.2 all-reduce.2
where the time goes:
time: 234 us; the launch traced here: 232 us
  waiting for transfers between devices  180 us (77%)
  between operations  23.5 us (10%)
  matrix products  14.4 us (6%)
  local copies, waits for them, and re-layouts  7.02 us (3%)
  other arithmetic  6.81 us (3%)
    ppermute x3, waiting for transfers between devices, shifted(): lax.ppermute(x, axis, [(i, (i + by) % devices) for i in range(devices)])  98.4 us
    psum x1, waiting for transfers between devices, from_root(): return lax.psum(block, axis)  81.1 us
    dot_general x4, matrix products, shards(): jnp.dot(left_tile, right_slab, preferred_element_type=jnp.float32)  14.4 us
    select_n x2, other arithmetic, from_root(): jnp.where(lax.axis_index(axis) == source, block, jnp.zeros_like(block))  6.8 us
  transfers between devices with their start and end apart: 4, of which 3 were waited for; matrix products, arithmetic and copies ran while one was open for 5% of the time, Pallas kernels for 0%

commit v1 on v0

v1 whole, which is shorter than its diff:
```python
import functools

import jax
import jax.numpy as jnp
from jax import lax
from jax.experimental import pallas as pl
from jax.experimental.pallas import tpu as pltpu
from jax.sharding import PartitionSpec as P

BLOCK = 128
STEPS = 4
GROUPS = 4
RUN_BITS = 2
RUN = 1 << RUN_BITS
LIST = 128

VMEM = pl.BlockSpec(memory_space=pltpu.VMEM)
SMEM = pl.BlockSpec(memory_space=pltpu.SMEM)
ANY = pl.BlockSpec(memory_space=pl.ANY)
SMALL = pl.CostEstimate(flops=1000, bytes_accessed=1000, transcendentals=0)
LARGE = pl.CostEstimate(flops=10**10, bytes_accessed=40 * 2**20, transcendentals=0)


class Plan:
    def __init__(self, row_count, col_count, tile_rows, tile_width):
        self.row_count = row_count
        self.col_count = col_count
        self.tile_rows = tile_rows
        self.tile_width = tile_width
        self.row_blocks = tile_rows // BLOCK
        self.col_blocks = tile_width // BLOCK
        self.cells = self.row_blocks * self.col_blocks
        self.group = row_count // col_count
        self.cap = self.cells * 3 // 5
        self.piece = BLOCK // self.group
        self.held = max(1, STEPS // col_count)
        self.shifts = [
            [t for t in range(STEPS) if t % col_count == s]
            for s in range(min(col_count, STEPS))
        ]


def list_blocks(plan, mask, row0, col0, put, marks):
    together = 4

    def some_rows(m, count):
        cells = [(m * together + i, c) for i in range(together) for c in range(plan.col_blocks)]
        kept = [mask[row0 + r, col0 + c] for r, c in cells]
        for (r, c), one in zip(cells, kept):
            put(count, r, c)
            count = count + one
        return count

    counts = [jnp.int32(0)]
    for first, last in zip(marks[:-1], marks[1:]):
        counts.append(
            lax.fori_loop(first // together, last // together, some_rows, counts[-1])
        )
    return counts


def pack_kernel(plan, mask_any, tile_any, *refs):
    *outs, tile, mask, listed, tile_sems, mask_sem = refs
    grid_col = lax.axis_index("row")
    row0 = lax.axis_index("col") * plan.row_blocks
    col0 = grid_col * plan.col_blocks
    chunks = 6
    chunk_blocks = plan.row_blocks // chunks
    marks = [q * chunk_blocks for q in range(chunks + 1)]

    mask_copy = pltpu.make_async_copy(mask_any, mask, mask_sem)
    mask_copy.start()
    copies = []
    for q in range(chunks):
        rows = pl.ds(marks[q] * plan.group, chunk_blocks * plan.group)
        copy = pltpu.make_async_copy(tile_any.at[rows], tile.at[rows], tile_sems.at[q])
        copy.start()
        copies.append(copy)
    mask_copy.wait()

    def put(n, r, c):
        listed[n] = 4 * r + c

    counts = list_blocks(plan, mask, row0, col0, put, marks)
    place = lax.rem(grid_col, plan.group)
    parts = [jnp.bitwise_xor(place, k) for k in range(plan.group)]

    def one_block(n, carry):
        code = listed[n]
        top = lax.shift_right_logical(code, 2) * plan.group
        left = pl.multiple_of(jnp.bitwise_and(code, 3) * BLOCK, BLOCK)
        for k in range(plan.group):
            block = tile[top + parts[k], :, pl.ds(left, BLOCK)]
            outs[k % len(outs)][k // len(outs), n] = block
        return carry

    for q in range(chunks):
        copies[q].wait()
        lax.fori_loop(counts[q], counts[q + 1], one_block, 0)


def pack(plan, count, mask, tile):
    pieces = (plan.group // count, plan.cap, plan.piece, BLOCK)
    tile = tile.reshape(-1, plan.piece, plan.tile_width)
    return pl.pallas_call(
        functools.partial(pack_kernel, plan),
        out_shape=[jax.ShapeDtypeStruct(pieces, jnp.bfloat16)] * count,
        in_specs=[ANY, ANY],
        out_specs=[VMEM] * count,
        scratch_shapes=[
            pltpu.VMEM(tile.shape, jnp.bfloat16),
            pltpu.SMEM(mask.shape, jnp.int32),
            pltpu.SMEM((plan.cells,), jnp.int32),
            pltpu.SemaphoreType.DMA((6,)),
            pltpu.SemaphoreType.DMA,
        ],
        compiler_params=pltpu.CompilerParams(vmem_limit_bytes=60 * 2**20),
        name="pack",
    )(mask, tile)


def slabs_kernel(plan, mask, owner, tile, *refs):
    slabs = refs[: len(plan.shifts)]
    found, sems = refs[len(plan.shifts) :]
    grid_row = lax.axis_index("col")
    row0 = grid_row * plan.row_blocks
    col0 = lax.axis_index("row") * plan.col_blocks
    width = plan.tile_width
    wanted = []
    for s, steps in enumerate(plan.shifts):
        target = lax.rem(grid_row - s + plan.col_count, plan.col_count)
        for i, t in enumerate(steps):
            first = lax.rem(owner[target, t], plan.group)
            copy = pltpu.make_async_copy(
                tile.at[pl.ds(pl.multiple_of(first * width, width), width)],
                found.at[t],
                sems.at[t],
            )
            copy.start()
            wanted.append((s, i, t, first * plan.col_blocks, copy))
    for s, i, t, first, copy in wanted:
        copy.wait()
        for r in range(plan.col_blocks):
            for c in range(plan.col_blocks):
                kept = mask[row0 + first + r, col0 + c]
                block = found[t, r * BLOCK : (r + 1) * BLOCK, c * BLOCK : (c + 1) * BLOCK]
                to = i * width + r * BLOCK
                slabs[s][to : to + BLOCK, c * BLOCK : (c + 1) * BLOCK] = jnp.where(
                    kept == 1, block, jnp.zeros_like(block)
                )


def slabs_of(plan, mask, owner, tile):
    width = plan.tile_width
    return pl.pallas_call(
        functools.partial(slabs_kernel, plan),
        out_shape=[
            jax.ShapeDtypeStruct((len(s) * width, width), jnp.bfloat16) for s in plan.shifts
        ],
        in_specs=[SMEM, SMEM, ANY],
        out_specs=[VMEM] * len(plan.shifts),
        scratch_shapes=[
            pltpu.VMEM((STEPS, width, width), jnp.bfloat16),
            pltpu.SemaphoreType.DMA((STEPS,)),
        ],
        cost_estimate=SMALL,
        compiler_params=pltpu.CompilerParams(vmem_limit_bytes=8 * 2**20),
        name="slabs",
    )(mask, owner, tile)


def lists_kernel(plan, mask, owner, lists):
    grid_row = lax.axis_index("col")
    row0 = grid_row * plan.row_blocks
    for t in range(STEPS):

        def put(n, r, c):
            lists[t, n] = c * GROUPS * plan.row_blocks + r

        col0 = owner[grid_row, t] * plan.col_blocks
        count = list_blocks(plan, mask, row0, col0, put, [0, plan.row_blocks])[-1]
        lists[t, LIST - 1] = count


def lists_of(plan, mask, owner):
    return pl.pallas_call(
        functools.partial(lists_kernel, plan),
        out_shape=jax.ShapeDtypeStruct((STEPS, LIST), jnp.int32),
        in_specs=[SMEM, SMEM],
        out_specs=SMEM,
        cost_estimate=SMALL,
        compiler_params=pltpu.CompilerParams(vmem_limit_bytes=2 * 2**20),
        name="lists",
    )(mask, owner)


def counts_kernel(plan, branches, mask, owner, counts):
    grid_row = lax.axis_index("col")
    most = jnp.int32(0)
    chip_most = jnp.int32(0)
    for g in range(plan.col_count):
        kept = mask[g * plan.row_blocks : (g + 1) * plan.row_blocks, :]
        column = lax.broadcasted_iota(jnp.int32, kept.shape, 1)
        found = []
        for t in range(STEPS):
            col0 = owner[g, t] * plan.col_blocks
            inside = (column >= col0) & (column < col0 + plan.col_blocks)
            found.append(jnp.sum(jnp.where(inside, kept, 0)))

        @pl.when(grid_row == g)
        def _():
            for t in range(STEPS):
                counts[t] = found[t]

        for t in range(STEPS // 2):
            total = found[t] + found[t + 2]
            one_chip = jnp.bitwise_xor(owner[g, t], owner[g, t + 2]) == 1
            most = jnp.maximum(most, total)
            chip_most = jnp.maximum(chip_most, jnp.where(one_chip, total, 0))
    choice = jnp.int32(len(branches) - 1)
    for i, (capacity, chip_capacity) in reversed(list(enumerate(branches))):
        choice = jnp.where((most <= capacity) & (chip_most <= chip_capacity), i, choice)
    counts[STEPS] = choice


def counts_of(plan, branches, mask, owner):
    return pl.pallas_call(
        functools.partial(counts_kernel, plan, branches),
        out_shape=jax.ShapeDtypeStruct((STEPS + 1,), jnp.int32),
        in_specs=[VMEM, SMEM],
        out_specs=SMEM,
        cost_estimate=SMALL,
        compiler_params=pltpu.CompilerParams(vmem_limit_bytes=2 * 2**20),
        name="counts",
    )(mask, owner)


def copy_blocks(count, copy):
    def run(m, carry):
        for n in range(RUN):
            copy(jnp.minimum(m * RUN + n, count - 1))
        return carry

    lax.fori_loop(0, lax.shift_right_logical(count + RUN - 1, RUN_BITS), run, 0)


def used_tiles(plan, counts, owner):
    grid_row = lax.axis_index("col")
    grid_col = lax.axis_index("row")
    first = lax.rem(lax.div(grid_col, plan.group) + grid_row, 2)
    roots = [lax.rem(owner[grid_row, first + 2 * i], plan.group) for i in range(2)]
    blocks = [counts[first + 2 * i] for i in range(2)]
    return lax.rem(grid_col, plan.group), roots, blocks


def merge_kernel(plan, counts, owner, own, other, *refs):
    *outs, joint = refs
    place, roots, blocks = used_tiles(plan, counts, owner)
    core = jnp.bitwise_and(place, 1)
    lower = place - core
    at = jnp.int32(0)
    for i in range(2):
        count = jnp.where(
            roots[0] == lower + i, blocks[0], jnp.where(roots[1] == lower + i, blocks[1], 0)
        )
        for source, mine in ((own, core == i), (other, core != i)):

            def copy(n, source=source, at=at):
                for d in range(len(outs)):
                    joint[d, at + n] = source[d, n]

            copy_blocks(jnp.where(mine, count, 0), copy)
        at = at + count

    def some(n, carry):
        for d, out in enumerate(outs):
            out[n] = joint[d, n]
        return carry

    lax.fori_loop(0, outs[0].shape[0], some, 0)


def merge(plan, capacity, counts, owner, own, other):
    count = plan.group // 2
    shape = jax.ShapeDtypeStruct((capacity, plan.piece, BLOCK), jnp.bfloat16)
    return pl.pallas_call(
        functools.partial(merge_kernel, plan),
        out_shape=[shape] * count,
        in_specs=[SMEM, SMEM, VMEM, VMEM],
        out_specs=[VMEM] * count,
        scratch_shapes=[pltpu.VMEM((count, 2 * plan.cap, plan.piece, BLOCK), jnp.bfloat16)],
        compiler_params=pltpu.CompilerParams(vmem_limit_bytes=10 * 2**20),
        name="merge",
    )(counts, owner, own, other)


def take_kernel(plan, counts, owner, *refs):
    chips, outs, joint = refs[:-3], refs[-3:-1], refs[-1]
    place, roots, blocks = used_tiles(plan, counts, owner)
    at = jnp.int32(0)
    for i in range(2):
        root, other = roots[i], roots[1 - i]
        behind = (jnp.bitwise_and(root, 1) == 1) & (other == root - 1)
        start = jnp.where(behind, blocks[1 - i], 0)
        distance = lax.shift_right_logical(jnp.bitwise_xor(root, place), 1)
        for d, chip in enumerate(chips):

            def copy(n, chip=chip, at=at):
                joint[at + n] = chip[start + n]

            copy_blocks(jnp.where(distance == d, blocks[i], 0), copy)
        at = at + blocks[i]
    for out in outs:

        def some(m, carry, out=out):
            out[pl.ds(2 * m, 2)] = joint[pl.ds(2 * m, 2)]
            return carry

        lax.fori_loop(0, out.shape[0] // 2, some, 0)


def take(plan, sizes, counts, owner, chips):
    return pl.pallas_call(
        functools.partial(take_kernel, plan),
        out_shape=[
            jax.ShapeDtypeStruct((size, plan.piece, BLOCK), jnp.bfloat16) for size in sizes
        ],
        in_specs=[SMEM, SMEM] + [VMEM] * len(chips),
        out_specs=[VMEM] * len(sizes),
        scratch_shapes=[pltpu.VMEM((2 * plan.cap, plan.piece, BLOCK), jnp.bfloat16)],
        compiler_params=pltpu.CompilerParams(vmem_limit_bytes=8 * 2**20),
        name="take",
    )(counts, owner, *chips)


def pick_kernel(plan, lists, owner, *refs):
    pieces = refs[: plan.group]
    joint = refs[-1]
    outs = refs[plan.group : -1]
    grid_row = lax.axis_index("col")
    grid_col = lax.axis_index("row")
    mine = lax.div(grid_col, plan.group)
    place = lax.rem(grid_col, plan.group)
    first = lax.rem(mine - grid_row + plan.col_count, plan.col_count)
    at = jnp.int32(0)
    for i in range(plan.held):
        step = lax.rem(first + i * plan.col_count, STEPS)
        root = lax.rem(owner[grid_row, step], plan.group)
        for k, piece in enumerate(pieces):

            @pl.when(root == jnp.bitwise_xor(place, k))
            def _():
                joint[pl.ds(at, plan.cap)] = piece[0]

        at = at + lists[step, LIST - 1]
    low = 0
    for out in outs:
        out[...] = joint[low : low + out.shape[0]]
        low += out.shape[0]


def pick(plan, sizes, lists, owner, pieces):
    return pl.pallas_call(
        functools.partial(pick_kernel, plan),
        out_shape=[
            jax.ShapeDtypeStruct((size, plan.piece, BLOCK), jnp.bfloat16) for size in sizes
        ],
        in_specs=[SMEM, SMEM] + [VMEM] * plan.group,
        out_specs=[VMEM] * len(sizes),
        scratch_shapes=[
            pltpu.VMEM((plan.held * plan.cap, plan.piece, BLOCK), jnp.bfloat16),
        ],
        compiler_params=pltpu.CompilerParams(vmem_limit_bytes=8 * 2**20),
        name="pick",
    )(lists, owner, *pieces)


def stack_kernel(ranges, *refs):
    to = 0
    for ref, (low, count) in zip(refs, ranges):
        together = 2 if count % 2 == 0 else 1

        def some(m, carry, ref=ref, low=low, to=to, together=together):
            refs[-1][pl.ds(to + m * together, together)] = ref[
                pl.ds(low + m * together, together)
            ]
            return carry

        lax.fori_loop(0, count // together, some, 0)
        to += count


def stacked(*pieces):
    ranges = [(low, count) for _, low, count in pieces]
    rows = sum(count for _, count in ranges)
    first = pieces[0][0]
    return pl.pallas_call(
        functools.partial(stack_kernel, ranges),
        out_shape=jax.ShapeDtypeStruct((rows,) + first.shape[1:], first.dtype),
        in_specs=[VMEM] * len(pieces),
        out_specs=VMEM,
        cost_estimate=SMALL,
        compiler_params=pltpu.CompilerParams(vmem_limit_bytes=6 * 2**20),
        name="stacked",
    )(*[array for array, _, _ in pieces])


def blank(plan):
    together = 2 * plan.row_blocks

    def body(out):
        def some(m, carry):
            out[pl.ds(m * together, together)] = jnp.zeros((together,) + out.shape[1:], out.dtype)
            return carry

        lax.fori_loop(0, out.shape[0] // together, some, 0)

    parts = STEPS * plan.col_blocks * GROUPS * plan.row_blocks
    return pl.pallas_call(
        body,
        out_shape=jax.ShapeDtypeStruct((parts, plan.piece, BLOCK), jnp.bfloat16),
        out_specs=VMEM,
        cost_estimate=SMALL,
        compiler_params=pltpu.CompilerParams(vmem_limit_bytes=8 * 2**20),
        name="blank",
    )()


def part_kernel(plan, cut, places, lists_any, *refs):
    count = 1 + max(array for _, _, sources in places for both in sources for array, _ in both)
    arrays = refs[:count]
    slabs = refs[count]
    out, left, result, lists, sems, lists_sem = refs[-6:]
    grid_row = lax.axis_index("col")
    grid_col = lax.axis_index("row")
    width = plan.tile_width
    size = plan.piece
    stride = GROUPS * plan.row_blocks
    lists_copy = pltpu.make_async_copy(lists_any, lists, lists_sem)
    lists_copy.start()
    lists_copy.wait()
    for hop in sorted({place[1] for place in places}):
        chosen = range(len(places))
        level = jnp.bitwise_xor(lax.shift_right_logical(grid_col, 2), hop)
        for q in range(2):
            half = lax.shift_right_logical(jnp.bitwise_xor(level, 2 * q), 1)
            first = jnp.bitwise_xor(half, grid_row)
            joint = jnp.int32(0)
            for s in range(plan.held):
                step = first + 2 * s
                origin = (first * plan.held + s) * plan.col_blocks * stride
                blocks = lists[step, LIST - 1]
                split = jnp.minimum(blocks, jnp.maximum(cut - joint, 0))

                def run(m, carry, part, begin, end, shift):
                    for n in range(RUN):
                        n = jnp.minimum(begin + m * RUN + n, end - 1)
                        to = origin + lists[step, n]
                        for i in chosen:
                            array, base = places[i][2][q][part]
                            left[to + i * plan.row_blocks] = arrays[array][n + (base + shift)]
                    return carry

                for part, begin, end, shift in (
                    (0, 0, split, joint),
                    (1, split, blocks, joint - cut),
                ):
                    lax.fori_loop(
                        0,
                        lax.shift_right_logical(end - begin + RUN - 1, RUN_BITS),
                        functools.partial(run, part=part, begin=begin, end=end, shift=shift),
                        0,
                    )
                joint = joint + blocks

    hop = places[0][1]

    def finished(i):
        e = jnp.bitwise_xor(jnp.bitwise_and(grid_col, 7), 4 * hop + i)
        return pltpu.make_async_copy(
            result.at[i],
            out.at[:, pl.ds(pl.multiple_of(e * size, size), size), :],
            sems.at[i],
        )

    def one_group(i, carry):
        columns = [
            left[pl.ds(k * stride + i * plan.row_blocks, plan.row_blocks)].reshape(-1, BLOCK)
            for k in range(STEPS * plan.col_blocks)
        ]
        product = jnp.dot(
            jnp.concatenate(columns, axis=1), slabs[...], preferred_element_type=jnp.float32
        )
        result[i] = product.reshape(plan.row_blocks, size, width)
        finished(i).start()
        return carry

    lax.fori_loop(0, len(places), one_group, 0)
    for i in range(len(places)):
        finished(i).wait()


def part(plan, cut, lists, slabs, places, left, out):
    arrays = []

    def number(x):
        for i, array in enumerate(arrays):
            if array is x:
                return i
        arrays.append(x)
        return len(arrays) - 1

    places = [
        (flip, hop, [[(number(x), base) for x, base in both] for both in sources])
        for flip, hop, sources in places
    ]
    width = plan.tile_width
    shape = jax.ShapeDtypeStruct((plan.row_blocks, BLOCK, width), jnp.float32)
    extra = [left] if out is None else [left, out]
    count = 1 + len(arrays) + 1

    def body(*refs):
        part_kernel(plan, cut, places, *refs[:count], *refs[count + len(extra) :])

    return pl.pallas_call(
        body,
        out_shape=[shape, jax.ShapeDtypeStruct(left.shape, left.dtype)],
        in_specs=[ANY] + [VMEM] * (len(arrays) + 2) + [ANY] * (len(extra) - 1),
        out_specs=[ANY, VMEM],
        scratch_shapes=[
            pltpu.VMEM((len(places), plan.row_blocks, plan.piece, width), jnp.float32),
            pltpu.SMEM((STEPS, LIST), jnp.int32),
            pltpu.SemaphoreType.DMA((len(places),)),
            pltpu.SemaphoreType.DMA,
        ],
        input_output_aliases={count: 1} if out is None else {count: 1, count + 1: 0},
        cost_estimate=SMALL,
        compiler_params=pltpu.CompilerParams(vmem_limit_bytes=20 * 2**20),
        name="part",
    )(lists, *arrays, slabs, *extra)


def flipped(x, count, bits):
    return lax.ppermute(x, "row", [(i, i ^ bits) for i in range(count)])


def by_exchange(plan, lists, slabs, own, own_u):
    slabs = list(slabs)
    move = functools.partial(flipped, count=plan.row_count)
    tied = lambda *xs: lax.optimization_barrier(xs)
    u = own_u.shape[0]
    v = own.shape[0] - u
    slabs[1] = lax.ppermute(slabs[1], "col", [(0, 1), (1, 0)])
    far_u, near_u, own_x = move(own_u, bits=8), move(own_u, bits=4), move(own, bits=2)
    own_x, near_u, far_u, left, slabs[1] = tied(own_x, near_u, far_u, blank(plan), slabs[1])

    own_w = stacked((own, u, v), (own_x, u, v))
    far_w = move(own_w, bits=8)
    last_near = move(stacked((far_u, 0, u), (own_w, 0, 2 * v)), bits=4)
    near_far_x = move(stacked((near_u, 0, u), (far_u, 0, u)), bits=2)
    near_far_x, last_near, far_w = tied(near_far_x, last_near, far_w)

    last_xu = move(stacked((last_near, 0, u)), bits=2)
    last_w = move(far_w, bits=4)
    core = move(
        stacked(
            (own, 0, u + v),
            (own_x, 0, u + v),
            (far_u, 0, u),
            (near_u, 0, u),
            (last_near, 0, u + 2 * v),
            (near_far_x, 0, 2 * u),
            (far_w, 0, 2 * v),
        ),
        bits=1,
    )
    slabs = [slab.reshape(-1, plan.piece, plan.tile_width) for slab in slabs]
    right = stacked(*[(slab, 0, slab.shape[0]) for slab in slabs])
    right = right.reshape(STEPS * plan.tile_width, plan.tile_width)
    multiply = functools.partial(part, plan, u, lists, right)
    there = 2 * (u + v)
    out, left = multiply(
        [
            (0, 0, [[(own, 0), (own, u)], [(far_u, 0), (far_w, 0)]]),
            (1, 0, [[(core, 0), (core, u)], [(core, there), (core, there + 5 * u + 2 * v)]]),
            (2, 0, [[(own_x, 0), (own_x, u)], [(near_far_x, u), (far_w, v)]]),
            (
                3,
                0,
                [
                    [(core, u + v), (core, 2 * u + v)],
                    [(core, there + 4 * u + 2 * v), (core, there + 5 * u + 3 * v)],
                ],
            ),
        ],
        left,
        None,
    )
    last_xu, last_w, out = tied(last_xu, last_w, out)
    last_core = move(stacked((last_xu, 0, u), (last_w, 0, 2 * v)), bits=1)
    out, left = multiply(
        [
            (0, 1, [[(near_u, 0), (last_near, u)], [(last_near, 0), (last_w, 0)]]),
            (
                1,
                1,
                [
                    [(core, there + u), (core, there + 3 * u)],
                    [(core, there + 2 * u), (last_core, u)],
                ],
            ),
            (2, 1, [[(near_far_x, 0), (last_near, u + v)], [(last_xu, 0), (last_w, v)]]),
            (
                3,
                1,
                [
                    [(core, there + 3 * u + 2 * v), (core, there + 3 * u + v)],
                    [(last_core, 0), (last_core, u + v)],
                ],
            ),
        ],
        left,
        out,
    )
    return out.reshape(plan.tile_rows, plan.tile_width)


def multiply_kernel(plan, rows, mask, owner, lists, lefts, *refs):
    slabs = refs[: len(plan.shifts)]
    out, left, right, counts = refs[len(plan.shifts) :]
    grid_row = lax.axis_index("col")
    row0 = grid_row * plan.row_blocks
    width = plan.tile_width
    size = plan.piece

    @pl.when(pl.program_id(0) == 0)
    def _():
        for s, steps in enumerate(plan.shifts):
            for i, t in enumerate(steps):
                right[t * width : (t + 1) * width, :] = slabs[s][i * width : (i + 1) * width, :]
        for t in range(STEPS):
            counts[t] = sum(
                (lists[i, LIST - 1] for i in range(t % plan.col_count, t, plan.col_count)),
                jnp.int32(0),
            )

    def one_row(r, carry):
        block_row = row0 + pl.program_id(0) * rows + r
        for t in range(STEPS):
            root = owner[grid_row, t]
            group = lax.rem(grid_row + t, plan.col_count)
            for c in range(plan.col_blocks):
                kept = mask[block_row, root * plan.col_blocks + c]
                at = t * width + c * BLOCK

                @pl.when(kept == 1)
                def _():
                    have = counts[t]
                    for e in range(plan.group):
                        to = pl.multiple_of(r * BLOCK + e * size, size)
                        left[pl.ds(to, size), at : at + BLOCK] = lefts[
                            group * plan.group + e, have
                        ]
                    counts[t] = have + 1

                @pl.when(kept != 1)
                def _():
                    left[pl.ds(pl.multiple_of(r * BLOCK, BLOCK), BLOCK), at : at + BLOCK] = (
                        jnp.zeros((BLOCK, BLOCK), jnp.bfloat16)
                    )

        return carry

    lax.fori_loop(0, rows, one_row, 0)
    out[...] = jnp.dot(left[...], right[...], preferred_element_type=jnp.float32)


def multiply(plan, mask, owner, lists, lefts, slabs):
    rows = 4
    width = plan.tile_width
    return pl.pallas_call(
        functools.partial(multiply_kernel, plan, rows),
        grid=(plan.row_blocks // rows,),
        out_shape=jax.ShapeDtypeStruct((plan.tile_rows, width), jnp.float32),
        in_specs=[SMEM, SMEM, SMEM] + [VMEM] * (1 + len(slabs)),
        out_specs=pl.BlockSpec((rows * BLOCK, width), lambda i: (i, 0)),
        scratch_shapes=[
            pltpu.VMEM((rows * BLOCK, STEPS * width), jnp.bfloat16),
            pltpu.VMEM((STEPS * width, width), jnp.bfloat16),
            pltpu.SMEM((STEPS,), jnp.int32),
        ],
        compiler_params=pltpu.CompilerParams(vmem_limit_bytes=32 * 2**20),
        name="multiply",
    )(mask, owner, lists, lefts, *slabs)


def shards(density, block_mask, owner):
    row_count = lax.axis_size("row")
    col_count = lax.axis_size("col")
    plan = Plan(row_count, col_count, *density.shape)
    owner = owner.T
    most = plan.held * plan.cap
    most = plan.held * plan.cap
    if (row_count, col_count) == (16, 2):
        own, other = pack(plan, 2, block_mask, density)
        other = flipped(other, row_count, 1)
        small, middle = most * 5 // 16 * 2 + 2, most * 3 // 8 * 2
        sizes = [
            (small, plan.cap),
            (middle, plan.cap),
            (middle, middle),
            (most, plan.cap),
            (most, most),
        ]
        counts = counts_of(plan, sizes, block_mask, owner)

        def branch(capacity, chip_capacity):
            cut = capacity * 3 // 8 * 2

            def run(own, other, counts, owner, block_mask, density):
                chips = list(merge(plan, chip_capacity, counts, owner, own, other))
                for d in (3, 1, 2):
                    chips[d] = flipped(chips[d], row_count, 2 * d)
                slabs = slabs_of(plan, block_mask, owner, density)
                *slabs, block_mask = lax.optimization_barrier((*slabs, block_mask))
                lists = lists_of(plan, block_mask, owner)
                chips[3], *chips[:3], slabs, lists = lax.optimization_barrier(
                    (chips[3], *chips[:3], slabs, lists)
                )
                held = take(plan, [capacity, cut], counts, owner, chips)
                return by_exchange(plan, lists, slabs, *held)

            return run

        branches = [branch(*size) for size in sizes]
        return lax.switch(
            counts[STEPS], branches, own, other, counts, owner, block_mask, density
        )

    pieces = list(pack(plan, plan.group, block_mask, density))
    for k in range(1, plan.group):
        pieces[k] = flipped(pieces[k], row_count, k)
    lists = lists_of(plan, block_mask, owner)
    (held,) = pick(plan, [most], lists, owner, pieces)
    lefts = lax.all_gather(held, "row")
    slabs = [
        lax.ppermute(slab, "col", [(i, (i - s) % col_count) for i in range(col_count)])
        for s, slab in enumerate(slabs_of(plan, block_mask, owner, density))
    ]
    return multiply(plan, block_mask, owner, lists, lefts, slabs)


def solution(mesh):
    placed = (P("col", "row"), P(), P())
    return jax.shard_map(
        shards, mesh=mesh, in_specs=placed, out_specs=P("col", "row"), check_vma=False
    )
```

time: 234 us -> 74.1 us (0.32); the launches traced: 232 us -> 75.1 us
  waiting for transfers between devices: 180 us -> 31.5 us
  Pallas kernels: 0 us -> 28.1 us
  between operations: 23.5 us -> 0.85 us
  matrix products: 14.4 us -> 0 us
  starting transfers between devices: 0.68 us -> 13.4 us
  other arithmetic: 6.81 us -> 0 us
  local copies, waits for them, and re-layouts: 7.02 us -> 0.65 us
    psum x1 -> x0, waiting for transfers between devices: 81.1 us -> none  [from_root(): return lax.psum(block, axis)]
    ppermute x3 -> x15, waiting for transfers between devices: 98.4 us -> 31.5 us  [the longest x14 31.5 us: flipped(): return lax.ppermute(x, 'row', [(i, i ^ bits) for i in range(count)])]
    pallas_call x0 -> x16, Pallas kernels: none -> 28.1 us  [the longest x2 11.3 us: part(): pl.pallas_call(body, out_shape=[shape, jax.ShapeDtypeStruct(left.shape, l...]
    dot_general x4 -> x0, matrix products: 14.4 us -> none  [shards(): jnp.dot(left_tile, right_slab, preferred_element_type=jnp.float32)]
    ppermute x3 -> x15, starting transfers between devices: 0.68 us -> 13.4 us  [the longest x14 13.4 us: flipped(): return lax.ppermute(x, 'row', [(i, i ^ bits) for i in range(count)])]
    select_n x2 -> x0, other arithmetic: 6.8 us -> none  [from_root(): jnp.where(lax.axis_index(axis) == source, block, jnp.zeros_like(block))]
    unnamed x8 -> x0, local copies, waits for them, and re-layouts: 4.37 us -> none
  transfers between devices with their start and end apart: 4 -> 15, of which waited for: 3 -> 7; matrix products, arithmetic and copies ran while one was open for 5% -> 1% of each run, Pallas kernels for 0% -> 21%
where the time goes in v1:
time: 74.1 us; the launch traced here: 75.1 us
  waiting for transfers between devices  31.5 us (43%)
  Pallas kernels  28.1 us (38%)
  starting transfers between devices  13.4 us (18%)
  between operations  0.85 us (1%)
    ppermute x14, waiting for transfers between devices, flipped(): return lax.ppermute(x, 'row', [(i, i ^ bits) for i in range(count)])  31.5 us
    ppermute x14, starting transfers between devices, flipped(): return lax.ppermute(x, 'row', [(i, i ^ bits) for i in range(count)])  13.4 us
    pallas_call x2, Pallas kernels, part(): pl.pallas_call(body, out_shape=[shape, jax.ShapeDtypeStruct(left.shape, l...  11.3 us
    pallas_call x7, Pallas kernels, stacked(): pl.pallas_call(functools.partial(stack_kernel, ranges), out_shape=jax.Sha...  3.32 us
    pallas_call x1, Pallas kernels, pack(): pl.pallas_call(functools.partial(pack_kernel, plan), out_shape=[jax.Shape...  3.19 us
    pallas_call x1, Pallas kernels, lists_of(): pl.pallas_call(functools.partial(lists_kernel, plan), out_shape=jax.Shape...  2.95 us
    pallas_call x1, Pallas kernels, slabs_of(): pl.pallas_call(functools.partial(slabs_kernel, plan), out_shape=[jax.Shap...  2.44 us
    pallas_call x1, Pallas kernels, counts_of(): pl.pallas_call(functools.partial(counts_kernel, plan, branches), out_shap...  1.57 us
  transfers between devices with their start and end apart: 15, of which 7 were waited for; matrix products, arithmetic and copies ran while one was open for 1% of the time, Pallas kernels for 21%

profile of v1, /device:TPU:13, one launch (start us, length us, event | category | flops | bytes accessed | tf_op | source)
XLA Modules:
  0.0 75.1 jit_solution(10449394838660978990)
XLA Ops:
  0.0 3.2 %pack.1 = (bf16[4,43,16,128]{3,2,1,0:T(8,128)(2,1)S(1)}, bf16[4,43,16,128]{3,2,1,0:T(8,128)(2,1)}) custom-call(s32[48,48]{1,0:T(8,128)} %mask_any.1, bf16[192,16,384]{2,1,0:T(8,128)(2,1)} %bitcast.43), custom_call_target="tpu_custom_call" | custom-call | tf_op jit(solution)/shard_map/pack/pallas_call | solution.py:105
  3.3 1.6 %counts.1 = s32[5]{0:T(128)S(1)} custom-call(s32[48,48]{1,0:T(8,128)} %mask_any.1, s32[2,4]{1,0:T(2,128)} %bitcast.44), custom_call_target="tpu_custom_call" | custom-call | flops 1000 | bytes 1000 | tf_op jit(solution)/shard_map/counts/pallas_call | solution.py:227
  4.8 0.6 slice.3
  6.1 68.8 %conditional.1 = (f32[3072,384]{1,0:T(8,128)}) conditional(s32[]{:T(128)} %bitcast.21, (s32[5]{0:T(128)S(1)}, s32[2,4]{1,0:T(2,128)}, bf16[4,43,16,128]{3,2,1,0:T(8,128)(2,1)S(1)}, bf16[4,43,16,128]{3,2,1,0:T(8,128)(2,1)S(1)}, s32[48,48]{1,0:T(8,128)}, /*index=5*/bf16[3072,384]{1,0:T(8,128)(2,1)}) %tuple.56, ...), branch_computations={%region_0.0_spmd, %region_1.0_spmd, %region_2.0_spmd, %region_3.0_... | conditional | flops 12000 | bytes 27734296 | solution.py:736
  6.2 1.3 %merge.8 = (bf16[43,16,128]{2,1,0:T(8,128)(2,1)S(1)}, bf16[43,16,128]{2,1,0:T(8,128)(2,1)S(1)}, bf16[43,16,128]{2,1,0:T(8,128)(2,1)S(1)}, bf16[43,16,128]{2,1,0:T(8,128)(2,1)S(1)}) custom-call(s32[5]{0:T(128)S(1)} %get-tuple-element.185.counts, s32[2,4]{1,0:T(2,128)} %get-tuple-element.186.owner, bf16[4,43,16,128]{3,2,1,0:T(8,128)(2,1)S(1)} %get-tuple-element.187.own, ...), custom_call_target="tpu_custom_call" | custom-call | tf_op jit(solution)/shard_map/cond/branch_3_fun/merge/pallas_call | solution.py:286
  7.5 1.4 %collective-permute-start.42 = (bf16[43,16,128]{2,1,0:T(8,128)(2,1)S(1)}, bf16[43,16,128]{2,1,0:T(8,128)(2,1)S(1)}, u32[]{:S(2)}, u32[]{:S(2)}) collective-permute-start(bf16[43,16,128]{2,1,0:T(8,128)(2,1)S(1)} %get-tuple-element.189), channel_id=1, source_target_pairs={{0,12},{2,14},{4,8},{6,10},{8,4},{10,6},{12,0},{14,2},{16,28},{18,... | collective-permute-start | bytes 528392 | tf_op jit(solution)/shard_map/cond/branch_3_fun/ppermute | solution.py:544
  8.8 0.7 collective-permute-start.43
  9.6 1.1 %collective-permute-start.44 = (bf16[43,16,128]{2,1,0:T(8,128)(2,1)S(1)}, bf16[43,16,128]{2,1,0:T(8,128)(2,1)S(1)}, u32[]{:S(2)}, u32[]{:S(2)}) collective-permute-start(bf16[43,16,128]{2,1,0:T(8,128)(2,1)S(1)} %get-tuple-element.192), channel_id=1, source_target_pairs={{0,8},{2,10},{4,12},{6,14},{8,0},{10,2},{12,4},{14,6},{16,24},{18,... | collective-permute-start | bytes 528392 | tf_op jit(solution)/shard_map/cond/branch_3_fun/ppermute | solution.py:544
  10.7 2.4 %slabs.8 = (bf16[768,384]{1,0:T(8,128)(2,1)S(1)}, bf16[768,384]{1,0:T(8,128)(2,1)S(1)}) custom-call(s32[48,48]{1,0:T(8,128)} %get-tuple-element.199.mask, s32[2,4]{1,0:T(2,128)} %get-tuple-element.186.owner, bf16[3072,384]{1,0:T(8,128)(2,1)} %get-tuple-element.194.tile), custom_call_target="tpu_custom_call" | custom-call | flops 1000 | bytes 1000 | tf_op jit(solution)/shard_map/cond/branch_3_fun/slabs/pallas_call | solution.py:155
  13.1 3.0 %lists.8.refs_0_ = s32[4,128]{1,0:T(4,128)S(1)} custom-call(s32[48,48]{1,0:T(8,128)} %get-tuple-element.199.mask, s32[2,4]{1,0:T(2,128)} %get-tuple-element.186.owner), custom_call_target="tpu_custom_call" | custom-call | flops 1000 | bytes 1000 | tf_op jit(solution)/shard_map/cond/branch_3_fun/lists/pallas_call | solution.py:186
  16.1 2.5 %collective-permute-done.43.refs_1_ = bf16[43,16,128]{2,1,0:T(8,128)(2,1)S(1)} collective-permute-done((bf16[43,16,128]{2,1,0:T(8,128)(2,1)S(1)}, bf16[43,16,128]{2,1,0:T(8,128)(2,1)S(1)}, u32[]{:S(2)}, u32[]{:S(2)}) %collective-permute-start.43) | collective-permute-done | bytes 176160 | tf_op jit(solution)/shard_map/cond/branch_3_fun/ppermute | solution.py:544
  18.6 0.5 collective-permute-done.44.refs_2_
  19.1 1.4 %take.8 = (bf16[86,16,128]{2,1,0:T(8,128)(2,1)S(1)}, bf16[64,16,128]{2,1,0:T(8,128)(2,1)S(1)}) custom-call(s32[5]{0:T(128)S(1)} %get-tuple-element.185.counts, s32[2,4]{1,0:T(2,128)} %get-tuple-element.186.owner, bf16[43,16,128]{2,1,0:T(8,128)(2,1)S(1)} %get-tuple-element.201.refs_0_, bf16[43,16,128]{2,1,0:T(8,128)(2,1)S(1)} %collective-permute-done.43.refs_1_, ...), custom_call_target="tpu_custom_call" | custom-call | tf_op jit(solution)/shard_map/cond/branch_3_fun/take/pallas_call | solution.py:323
  20.6 2.5 %collective-permute-start.47 = (bf16[64,16,128]{2,1,0:T(8,128)(2,1)S(1)}, bf16[64,16,128]{2,1,0:T(8,128)(2,1)S(1)}, u32[]{:S(2)}, u32[]{:S(2)}) collective-permute-start(bf16[64,16,128]{2,1,0:T(8,128)(2,1)S(1)} %get-tuple-element.206), channel_id=1, source_target_pairs={{0,16},{2,18},{4,20},{6,22},{8,24},{10,26},{12,28},{14,30},{16,0},... | collective-permute-start | bytes 786440 | tf_op jit(solution)/shard_map/cond/branch_3_fun/ppermute | solution.py:544
  23.1 1.1 %collective-permute-start.46 = (bf16[64,16,128]{2,1,0:T(8,128)(2,1)S(1)}, bf16[64,16,128]{2,1,0:T(8,128)(2,1)S(1)}, u32[]{:S(2)}, u32[]{:S(2)}) collective-permute-start(bf16[64,16,128]{2,1,0:T(8,128)(2,1)S(1)} %get-tuple-element.206), channel_id=1, source_target_pairs={{0,8},{2,10},{4,12},{6,14},{8,0},{10,2},{12,4},{14,6},{16,24},{18,... | collective-permute-start | bytes 786440 | tf_op jit(solution)/shard_map/cond/branch_3_fun/ppermute | solution.py:544
  24.2 0.6 blank.8.refs_8_
  24.9 9.0 %collective-permute-done.47.refs_1_.refs_0_.refs_2_ = bf16[64,16,128]{2,1,0:T(8,128)(2,1)S(1)} collective-permute-done((bf16[64,16,128]{2,1,0:T(8,128)(2,1)S(1)}, bf16[64,16,128]{2,1,0:T(8,128)(2,1)S(1)}, u32[]{:S(2)}, u32[]{:S(2)}) %collective-permute-start.47) | collective-permute-done | bytes 262176 | tf_op jit(solution)/shard_map/cond/branch_3_fun/ppermute | solution.py:544
  33.9 1.3 %collective-permute-done.46.refs_0_.refs_3_.refs_1_ = bf16[64,16,128]{2,1,0:T(8,128)(2,1)S(1)} collective-permute-done((bf16[64,16,128]{2,1,0:T(8,128)(2,1)S(1)}, bf16[64,16,128]{2,1,0:T(8,128)(2,1)S(1)}, u32[]{:S(2)}, u32[]{:S(2)}) %collective-permute-start.46) | collective-permute-done | bytes 262176 | tf_op jit(solution)/shard_map/cond/branch_3_fun/ppermute | solution.py:544
  35.2 0.4 stacked.56
  35.6 0.7 collective-permute-start.49
  36.4 0.3 stacked.58
  36.7 0.9 %collective-permute-start.50 = (bf16[108,16,128]{2,1,0:T(8,128)(2,1)S(1)}, bf16[108,16,128]{2,1,0:T(8,128)(2,1)S(1)}, u32[]{:S(2)}, u32[]{:S(2)}) collective-permute-start(bf16[108,16,128]{2,1,0:T(8,128)(2,1)S(1)} %stacked.58), channel_id=1, source_target_pairs={{0,8},{2,10},{4,12},{6,14},{8,0},{10,2},{12,4},{14,6},{16,24},{18,... | collective-permute-start | bytes 1327112 | tf_op jit(solution)/shard_map/cond/branch_3_fun/ppermute | solution.py:544
  37.6 2.3 %collective-permute-start.51 = (bf16[44,16,128]{2,1,0:T(8,128)(2,1)S(1)}, bf16[44,16,128]{2,1,0:T(8,128)(2,1)S(1)}, u32[]{:S(2)}, u32[]{:S(2)}) collective-permute-start(bf16[44,16,128]{2,1,0:T(8,128)(2,1)S(1)} %stacked.57.refs_1_), channel_id=1, source_target_pairs={{0,16},{2,18},{4,20},{6,22},{8,24},{10,26},{12,28},{14,30},{16,0},... | collective-permute-start | bytes 540680 | tf_op jit(solution)/shard_map/cond/branch_3_fun/ppermute | solution.py:544
  39.9 13.6 %collective-permute-done.51.refs_6_.refs_3_ = bf16[44,16,128]{2,1,0:T(8,128)(2,1)S(1)} collective-permute-done((bf16[44,16,128]{2,1,0:T(8,128)(2,1)S(1)}, bf16[44,16,128]{2,1,0:T(8,128)(2,1)S(1)}, u32[]{:S(2)}, u32[]{:S(2)}) %collective-permute-start.51) | collective-permute-done | bytes 180256 | tf_op jit(solution)/shard_map/cond/branch_3_fun/ppermute | solution.py:544
  53.5 1.8 %stacked.60 = bf16[580,16,128]{2,1,0:T(8,128)(2,1)S(1)} custom-call(bf16[86,16,128]{2,1,0:T(8,128)(2,1)S(1)} %get-tuple-element.205.refs_0_.refs_1_, bf16[86,16,128]{2,1,0:T(8,128)(2,1)S(1)} %collective-permute-done.45.refs_1_.refs_5_, bf16[64,16,128]{2,1,0:T(8,128)(2,1)S(1)} %collective-permute-done.47.refs_1_.refs_0_.refs_2_, ...), custom_call_target="tpu_custom_call" | custom-call | flops 1000 | bytes 1000 | tf_op jit(solution)/shard_map/cond/branch_3_fun/stacked/pallas_call | solution.py:397
  55.3 1.4 %collective-permute-start.54 = (bf16[580,16,128]{2,1,0:T(8,128)(2,1)S(1)}, bf16[580,16,128]{2,1,0:T(8,128)(2,1)S(1)}, u32[]{:S(2)}, u32[]{:S(2)}) collective-permute-start(bf16[580,16,128]{2,1,0:T(8,128)(2,1)S(1)} %stacked.60), channel_id=1, source_target_pairs={{0,2},{2,0},{4,6},{6,4},{8,10},{10,8},{12,14},{14,12},{16,18},{18,... | collective-permute-start | bytes 7127048 | tf_op jit(solution)/shard_map/cond/branch_3_fun/ppermute | solution.py:544
  57.0 0.5 collective-permute-start.53
  57.8 3.1 %collective-permute-done.54.refs_4_ = bf16[580,16,128]{2,1,0:T(8,128)(2,1)S(1)} collective-permute-done((bf16[580,16,128]{2,1,0:T(8,128)(2,1)S(1)}, bf16[580,16,128]{2,1,0:T(8,128)(2,1)S(1)}, u32[]{:S(2)}, u32[]{:S(2)}) %collective-permute-start.54) | collective-permute-done | bytes 2375712 | tf_op jit(solution)/shard_map/cond/branch_3_fun/ppermute | solution.py:544
  60.9 5.6 %part.16 = (f32[24,128,384]{2,1,0:T(8,128)}, bf16[1152,16,128]{2,1,0:T(8,128)(2,1)S(1)}) custom-call(s32[4,128]{1,0:T(4,128)S(1)} %lists.8.refs_0_, bf16[86,16,128]{2,1,0:T(8,128)(2,1)S(1)} %get-tuple-element.205.refs_0_.refs_1_, bf16[64,16,128]{2,1,0:T(8,128)(2,1)S(1)} %collective-permute-done.47.refs_1_.refs_0_.refs_2_, ...), custom_call_target="tpu_custom_call", output_to_operand_aliasing={{1}: (8, {})} | custom-call | flops 1000 | bytes 1000 | tf_op jit(solution)/shard_map/cond/branch_3_fun/part/pallas_call | solution.py:525
  66.9 0.4 collective-permute-start.55
  67.3 1.4 %collective-permute-done.55.refs_5_ = bf16[108,16,128]{2,1,0:T(8,128)(2,1)S(1)} collective-permute-done((bf16[108,16,128]{2,1,0:T(8,128)(2,1)S(1)}, bf16[108,16,128]{2,1,0:T(8,128)(2,1)S(1)}, u32[]{:S(2)}, u32[]{:S(2)}) %collective-permute-start.55) | collective-permute-done | bytes 442400 | tf_op jit(solution)/shard_map/cond/branch_3_fun/ppermute | solution.py:544
  68.8 5.7 %part.17 = (f32[24,128,384]{2,1,0:T(8,128)}, bf16[1152,16,128]{2,1,0:T(8,128)(2,1)S(1)}) custom-call(s32[4,128]{1,0:T(4,128)S(1)} %lists.8.refs_0_, bf16[64,16,128]{2,1,0:T(8,128)(2,1)S(1)} %collective-permute-done.46.refs_0_.refs_3_.refs_1_, ...), custom_call_target="tpu_custom_call", output_to_operand_aliasing={{1}: (9, {}), {0}: (10, {})} | custom-call | flops 1000 | bytes 1000 | tf_op jit(solution)/shard_map/cond/branch_3_fun/part/pallas_call | solution.py:525
  (16 shorter events, 1.1 us)
Async XLA Ops:
  3.2 2.9 %collective-permute-start.70 = (bf16[4,43,16,128]{3,2,1,0:T(8,128)(2,1)}, bf16[4,43,16,128]{3,2,1,0:T(8,128)(2,1)S(1)}, u32[]{:S(2)}, u32[]{:S(2)}) collective-permute-start(bf16[4,43,16,128]{3,2,1,0:T(8,128)(2,1)} %get-tuple-element.264), channel_id=1, source_target_pairs={{0,2},{2,0},{4,6},{6,4},{8,10},{10,8},{12,14},{14,12},{16,18},{18,... | collective-permute-start | bytes 2113544 | tf_op jit(solution)/shard_map/ppermute | solution.py:544
  7.5 8.6 %collective-permute-start.42 = (bf16[43,16,128]{2,1,0:T(8,128)(2,1)S(1)}, bf16[43,16,128]{2,1,0:T(8,128)(2,1)S(1)}, u32[]{:S(2)}, u32[]{:S(2)}) collective-permute-start(bf16[43,16,128]{2,1,0:T(8,128)(2,1)S(1)} %get-tuple-element.189), channel_id=1, source_target_pairs={{0,12},{2,14},{4,8},{6,10},{8,4},{10,6},{12,0},{14,2},{16,28},{18,... | collective-permute-start | bytes 528392 | tf_op jit(solution)/shard_map/cond/branch_3_fun/ppermute | solution.py:544
  8.8 9.8 %collective-permute-start.43 = (bf16[43,16,128]{2,1,0:T(8,128)(2,1)S(1)}, bf16[43,16,128]{2,1,0:T(8,128)(2,1)S(1)}, u32[]{:S(2)}, u32[]{:S(2)}) collective-permute-start(bf16[43,16,128]{2,1,0:T(8,128)(2,1)S(1)} %get-tuple-element.191), channel_id=1, source_target_pairs={{0,4},{2,6},{4,0},{6,2},{8,12},{10,14},{12,8},{14,10},{16,20},{18,... | collective-permute-start | bytes 528392 | tf_op jit(solution)/shard_map/cond/branch_3_fun/ppermute | solution.py:544
  9.6 9.5 %collective-permute-start.44 = (bf16[43,16,128]{2,1,0:T(8,128)(2,1)S(1)}, bf16[43,16,128]{2,1,0:T(8,128)(2,1)S(1)}, u32[]{:S(2)}, u32[]{:S(2)}) collective-permute-start(bf16[43,16,128]{2,1,0:T(8,128)(2,1)S(1)} %get-tuple-element.192), channel_id=1, source_target_pairs={{0,8},{2,10},{4,12},{6,14},{8,0},{10,2},{12,4},{14,6},{16,24},{18,... | collective-permute-start | bytes 528392 | tf_op jit(solution)/shard_map/cond/branch_3_fun/ppermute | solution.py:544
  19.1 16.1 %collective-permute-start.48 = (bf16[768,384]{1,0:T(8,128)(2,1)S(1)}, bf16[768,384]{1,0:T(8,128)(2,1)S(1)}, u32[]{:S(2)}, u32[]{:S(2)}) collective-permute-start(bf16[768,384]{1,0:T(8,128)(2,1)S(1)} %get-tuple-element.207), channel_id=1, source_target_pairs={{0,1},{1,0},{2,3},{3,2},{4,5},{5,4},{6,7},{7,6},{8,9},{9,8},{10,11... | collective-permute-start | bytes 1769480 | tf_op jit(solution)/shard_map/cond/branch_3_fun/ppermute | solution.py:553
  20.5 14.7 %collective-permute-start.45 = (bf16[86,16,128]{2,1,0:T(8,128)(2,1)S(1)}, bf16[86,16,128]{2,1,0:T(8,128)(2,1)S(1)}, u32[]{:S(2)}, u32[]{:S(2)}) collective-permute-start(bf16[86,16,128]{2,1,0:T(8,128)(2,1)S(1)} %get-tuple-element.205.refs_0_.refs_1_), channel_id=1, source_target_pairs={{0,4},{2,6},{4,0},{6,2},{8,12},{10,14},{12,8},{14,10},{16,20},{18,... | collective-permute-start | bytes 1056776 | tf_op jit(solution)/shard_map/cond/branch_3_fun/ppermute | solution.py:544
  20.6 13.2 %collective-permute-start.47 = (bf16[64,16,128]{2,1,0:T(8,128)(2,1)S(1)}, bf16[64,16,128]{2,1,0:T(8,128)(2,1)S(1)}, u32[]{:S(2)}, u32[]{:S(2)}) collective-permute-start(bf16[64,16,128]{2,1,0:T(8,128)(2,1)S(1)} %get-tuple-element.206), channel_id=1, source_target_pairs={{0,16},{2,18},{4,20},{6,22},{8,24},{10,26},{12,28},{14,30},{16,0},... | collective-permute-start | bytes 786440 | tf_op jit(solution)/shard_map/cond/branch_3_fun/ppermute | solution.py:544
  23.1 12.1 %collective-permute-start.46 = (bf16[64,16,128]{2,1,0:T(8,128)(2,1)S(1)}, bf16[64,16,128]{2,1,0:T(8,128)(2,1)S(1)}, u32[]{:S(2)}, u32[]{:S(2)}) collective-permute-start(bf16[64,16,128]{2,1,0:T(8,128)(2,1)S(1)} %get-tuple-element.206), channel_id=1, source_target_pairs={{0,8},{2,10},{4,12},{6,14},{8,0},{10,2},{12,4},{14,6},{16,24},{18,... | collective-permute-start | bytes 786440 | tf_op jit(solution)/shard_map/cond/branch_3_fun/ppermute | solution.py:544
  35.6 17.9 %collective-permute-start.49 = (bf16[128,16,128]{2,1,0:T(8,128)(2,1)S(1)}, bf16[128,16,128]{2,1,0:T(8,128)(2,1)S(1)}, u32[]{:S(2)}, u32[]{:S(2)}) collective-permute-start(bf16[128,16,128]{2,1,0:T(8,128)(2,1)S(1)} %stacked.56), channel_id=1, source_target_pairs={{0,4},{2,6},{4,0},{6,2},{8,12},{10,14},{12,8},{14,10},{16,20},{18,... | collective-permute-start | bytes 1572872 | tf_op jit(solution)/shard_map/cond/branch_3_fun/ppermute | solution.py:544
  36.7 16.8 %collective-permute-start.50 = (bf16[108,16,128]{2,1,0:T(8,128)(2,1)S(1)}, bf16[108,16,128]{2,1,0:T(8,128)(2,1)S(1)}, u32[]{:S(2)}, u32[]{:S(2)}) collective-permute-start(bf16[108,16,128]{2,1,0:T(8,128)(2,1)S(1)} %stacked.58), channel_id=1, source_target_pairs={{0,8},{2,10},{4,12},{6,14},{8,0},{10,2},{12,4},{14,6},{16,24},{18,... | collective-permute-start | bytes 1327112 | tf_op jit(solution)/shard_map/cond/branch_3_fun/ppermute | solution.py:544
  37.6 15.9 %collective-permute-start.51 = (bf16[44,16,128]{2,1,0:T(8,128)(2,1)S(1)}, bf16[44,16,128]{2,1,0:T(8,128)(2,1)S(1)}, u32[]{:S(2)}, u32[]{:S(2)}) collective-permute-start(bf16[44,16,128]{2,1,0:T(8,128)(2,1)S(1)} %stacked.57.refs_1_), channel_id=1, source_target_pairs={{0,16},{2,18},{4,20},{6,22},{8,24},{10,26},{12,28},{14,30},{16,0},... | collective-permute-start | bytes 540680 | tf_op jit(solution)/shard_map/cond/branch_3_fun/ppermute | solution.py:544
  55.3 5.6 %collective-permute-start.54 = (bf16[580,16,128]{2,1,0:T(8,128)(2,1)S(1)}, bf16[580,16,128]{2,1,0:T(8,128)(2,1)S(1)}, u32[]{:S(2)}, u32[]{:S(2)}) collective-permute-start(bf16[580,16,128]{2,1,0:T(8,128)(2,1)S(1)} %stacked.60), channel_id=1, source_target_pairs={{0,2},{2,0},{4,6},{6,4},{8,10},{10,8},{12,14},{14,12},{16,18},{18,... | collective-permute-start | bytes 7127048 | tf_op jit(solution)/shard_map/cond/branch_3_fun/ppermute | solution.py:544
  56.9 9.7 %collective-permute-start.52 = (bf16[64,16,128]{2,1,0:T(8,128)(2,1)S(1)}, bf16[64,16,128]{2,1,0:T(8,128)(2,1)S(1)}, u32[]{:S(2)}, u32[]{:S(2)}) collective-permute-start(bf16[64,16,128]{2,1,0:T(8,128)(2,1)S(1)} %stacked.59), channel_id=1, source_target_pairs={{0,4},{2,6},{4,0},{6,2},{8,12},{10,14},{12,8},{14,10},{16,20},{18,... | collective-permute-start | bytes 786440 | tf_op jit(solution)/shard_map/cond/branch_3_fun/ppermute | solution.py:544
  57.0 9.6 %collective-permute-start.53 = (bf16[44,16,128]{2,1,0:T(8,128)(2,1)S(1)}, bf16[44,16,128]{2,1,0:T(8,128)(2,1)S(1)}, u32[]{:S(2)}, u32[]{:S(2)}) collective-permute-start(bf16[44,16,128]{2,1,0:T(8,128)(2,1)S(1)} %collective-permute-done.51.refs_6_.refs_3_), channel_id=1, source_target_pairs={{0,8},{2,10},{4,12},{6,14},{8,0},{10,2},{12,4},{14,6},{16,24},{18,... | collective-permute-start | bytes 540680 | tf_op jit(solution)/shard_map/cond/branch_3_fun/ppermute | solution.py:544
  66.9 1.9 %collective-permute-start.55 = (bf16[108,16,128]{2,1,0:T(8,128)(2,1)S(1)}, bf16[108,16,128]{2,1,0:T(8,128)(2,1)S(1)}, u32[]{:S(2)}, u32[]{:S(2)}) collective-permute-start(bf16[108,16,128]{2,1,0:T(8,128)(2,1)S(1)} %stacked.62), channel_id=1, source_target_pairs={{0,2},{2,0},{4,6},{6,4},{8,10},{10,8},{12,14},{14,12},{16,18},{18,... | collective-permute-start | bytes 1327112 | tf_op jit(solution)/shard_map/cond/branch_3_fun/ppermute | solution.py:544
